TPU v7x, 32 devices: a whole 2x2x4 slice. The times are simulated.
32 devices in a mesh: grp: 4 (over y, core), ctx: 8 (over z, x).
Axes of the slice: x: 2, y: 2, z: 4, core: 2. Of those that a mesh axis runs over, the one named last changes fastest.
Arguments:
- query_rows: bfloat16 [4, 1024, 4096], P('grp', 'ctx'), may hold values from -6 to 6
- key_rows: bfloat16 [4, 1024, 512], P('grp', 'ctx'), may hold values from -6 to 6
- value_rows: bfloat16 [4, 1024, 512], P('grp', 'ctx'), may hold values from -5 to 5
- output_rows: bfloat16 [4, 1024, 4096], P('grp', 'ctx'), may hold values from -4 to 4
- output_grad: bfloat16 [4, 1024, 4096], P('grp', 'ctx'), may hold values from -5 to 5
- loss_mask: int32 [4, 1024], P('grp', 'ctx'), may hold values from 0 to 1
- doc_lengths: int32 [4, 12], P('grp'), may hold values from 1 to 256, 1024 in all within a row
- balance_plan: int32 [4, 128], P('grp'), may hold values from 0 to 127, as said below
Outputs:
- query_grad: bfloat16 [4, 1024, 4096], P('grp', 'ctx')
- key_grad: bfloat16 [4, 1024, 512], P('grp', 'ctx')
- value_grad: bfloat16 [4, 1024, 512], P('grp', 'ctx')
Inputs may be any that keep to these rules, and one draw needn't show every extreme that they name: Each row is a permutation of 0 to 127. Span c of a sequence (its tokens c * 8 to c * 8 + 7) goes to index balance_plan // 16 of ctx; of the 16 spans of one index of ctx at most 2 go to the same index.
All inputs are finite; a program needn't handle non-finite values.
Results may differ from a plain program's by a relative error of at most 0.0051.
Values may be sent and summed in bfloat16 or wider, within the bound.
A program may use at most 128 MiB of HBM per device.

v0:
```python
import jax
import jax.numpy as jnp
from jax import lax
from jax.sharding import PartitionSpec as P

HD = 128
QH = 32
KVH = 4
SPAN = 8


NEGATIVE = -1e30


def key_block():
    return 512


def doc_index(positions, doc_ends):
    return jnp.sum((positions[:, None] >= doc_ends[None, :]).astype(jnp.int32), axis=1)


def visible(query_pos, query_doc, key_pos, doc_ends):
    key_doc = doc_index(key_pos, doc_ends)
    return (key_pos[None, :] <= query_pos[:, None]) & (key_doc[None, :] == query_doc[:, None])


def head_scores(q_heads, k_heads, scale_value):
    return (
        jnp.einsum("rgsd,ngd->gsrn", q_heads, k_heads, preferred_element_type=jnp.float32)
        * scale_value
    )


def over_blocks(function, folded, members):
    row_total = members[0].shape[0]
    block_rows = key_block()
    step_count = row_total // block_rows
    stacked = tuple(
        (member.reshape((step_count, block_rows) + member.shape[1:]) for member in members)
    )

    def advance(carried, scanned):
        block_index, pieces = scanned
        positions = block_index * block_rows + jnp.arange(block_rows, dtype=jnp.int32)
        return (function(carried, pieces, positions), None)

    result, unused = lax.scan(advance, folded, (jnp.arange(step_count, dtype=jnp.int32), stacked))
    return result


def stats_update(carried, k_heads, key_pos, context):
    q_heads, query_pos, query_doc, doc_ends, scale_value = context
    old_peak, running_sum = carried
    scores = head_scores(q_heads, k_heads, scale_value)
    visible_mask = visible(query_pos, query_doc, key_pos, doc_ends)
    scores = jnp.where(visible_mask, scores, NEGATIVE)
    new_peak = jnp.maximum(old_peak, jnp.max(scores, axis=-1))
    weights = jnp.where(visible_mask, jnp.exp(scores - new_peak[..., None]), 0.0)
    running_sum = running_sum * jnp.exp(old_peak - new_peak) + jnp.sum(weights, axis=-1)
    return (new_peak, running_sum)


def block_grads(context, k_heads, v_heads, key_pos):
    q_heads, g_heads, query_pos, query_doc, doc_ends, lse_rows, delta_heads, scale_value = context
    scores = head_scores(q_heads, k_heads, scale_value)
    visible_mask = visible(query_pos, query_doc, key_pos, doc_ends)
    probs_full = jnp.where(
        visible_mask, jnp.exp(jnp.where(visible_mask, scores - lse_rows[..., None], NEGATIVE)), 0.0
    )
    probs_half = probs_full.astype(jnp.bfloat16)
    dprobs = jnp.einsum("rgsd,ngd->gsrn", g_heads, v_heads, preferred_element_type=jnp.float32)
    dscores = (probs_full * (dprobs - delta_heads[..., None]) * scale_value).astype(jnp.bfloat16)
    query_part = jnp.einsum("gsrn,ngd->rgsd", dscores, k_heads, preferred_element_type=jnp.float32)
    key_part = jnp.einsum("gsrn,rgsd->ngd", dscores, q_heads, preferred_element_type=jnp.float32)
    value_part = jnp.einsum(
        "gsrn,rgsd->ngd", probs_half, g_heads, preferred_element_type=jnp.float32
    )
    return (query_part, key_part, value_part)


def row_delta(grad_local, output_local):
    local_rows = grad_local.shape[0]
    product = grad_local.astype(jnp.float32) * output_local.astype(jnp.float32)
    return jnp.sum(product.reshape(local_rows, QH, HD), axis=-1)


def shards(
    query_rows, key_rows, value_rows, output_rows, output_grad, loss_mask, doc_lengths, balance_plan
):
    devices = lax.axis_size("ctx")
    device = lax.axis_index("ctx")
    local_rows = query_rows.shape[1]
    per_device = local_rows // SPAN
    slot_count = (per_device + devices - 1) // devices
    group_size = QH // KVH
    scale_value = HD ** (-0.5)
    counted = jnp.sum(loss_mask.astype(jnp.float32))
    total_counted = lax.psum(counted, ("grp", "ctx"))
    factor = lax.axis_size("grp") * devices * local_rows / jnp.maximum(total_counted, 1.0)
    grad_masked = output_grad[0] * loss_mask[0][:, None].astype(jnp.bfloat16)
    plan_row = balance_plan[0]
    dest_all = plan_row // per_device
    dest_grid = dest_all.reshape(devices, per_device)
    earlier = jnp.arange(per_device)[None, :] < jnp.arange(per_device)[:, None]
    same_dest = dest_grid[:, :, None] == dest_grid[:, None, :]
    rank_all = jnp.sum((same_dest & earlier[None, :, :]).astype(jnp.int32), axis=2).reshape(-1)
    inverse = jnp.argsort(plan_row)
    handled = lax.dynamic_slice_in_dim(inverse, device * per_device, per_device)
    receive_index = handled // per_device * slot_count + jnp.take(rank_all, handled)
    send_dest = lax.dynamic_slice_in_dim(dest_all, device * per_device, per_device)
    send_rank = lax.dynamic_slice_in_dim(rank_all, device * per_device, per_device)
    send_index = send_dest * slot_count + send_rank

    def pack_rows(member):
        row_width = member.shape[-1]
        pieces = member.reshape(per_device, SPAN, row_width)
        buffer = jnp.zeros((devices * slot_count, SPAN, row_width), member.dtype)
        return buffer.at[send_index].set(pieces)

    def unpack(member):
        return jnp.take(member, receive_index, axis=0).reshape(local_rows, member.shape[-1])

    moved_query, moved_grad, moved_output = (
        lax.all_to_all(pack_rows(query_rows[0]), "ctx", split_axis=0, concat_axis=0, tiled=True),
        lax.all_to_all(pack_rows(grad_masked), "ctx", split_axis=0, concat_axis=0, tiled=True),
        lax.all_to_all(pack_rows(output_rows[0]), "ctx", split_axis=0, concat_axis=0, tiled=True),
    )
    delta_rows = row_delta(unpack(moved_grad), unpack(moved_output))
    q_local = unpack(moved_query)
    g_local = unpack(moved_grad)
    q_heads = q_local.reshape(local_rows, KVH, group_size, HD)
    g_heads = g_local.reshape(local_rows, KVH, group_size, HD)
    delta_heads = jnp.transpose(delta_rows).reshape(KVH, group_size, local_rows)
    query_pos = (handled[:, None] * SPAN + jnp.arange(SPAN, dtype=jnp.int32)[None, :]).reshape(
        local_rows
    )
    doc_ends = jnp.cumsum(doc_lengths[0])
    query_doc = doc_index(query_pos, doc_ends)
    stats_context = (q_heads, query_pos, query_doc, doc_ends, scale_value)
    stats_initial = (
        jnp.full((KVH, group_size, local_rows), NEGATIVE, jnp.float32),
        jnp.zeros((KVH, group_size, local_rows), jnp.float32),
    )

    def stats_step_rows(carried, members, positions):
        return stats_update(carried, members[0].reshape(-1, KVH, HD), positions, stats_context)

    peak_rows, sum_rows = over_blocks(
        stats_step_rows, stats_initial, (lax.all_gather(key_rows, "ctx", axis=1, tiled=True)[0],)
    )
    lse_rows = peak_rows + jnp.log(sum_rows)
    grad_context = (
        q_heads,
        g_heads,
        query_pos,
        query_doc,
        doc_ends,
        lse_rows,
        delta_heads,
        scale_value,
    )
    dq_zero = jnp.zeros((local_rows, KVH, group_size, HD), jnp.float32)
    seq_total = local_rows * devices
    grads_initial = (
        dq_zero,
        jnp.zeros((seq_total, KVH, HD), jnp.float32),
        jnp.zeros((seq_total, KVH, HD), jnp.float32),
    )

    def grads_step_rows(carried, members, positions):
        dq_acc, dk_all, dv_all = carried
        k_heads = members[0].reshape(-1, KVH, HD)
        v_heads = members[1].reshape(-1, KVH, HD)
        query_part, key_part, value_part = block_grads(grad_context, k_heads, v_heads, positions)
        first_row = positions[0]
        old_keys = lax.dynamic_slice_in_dim(dk_all, first_row, key_part.shape[0], 0)
        dk_all = lax.dynamic_update_slice_in_dim(dk_all, old_keys + key_part, first_row, 0)
        old_values = lax.dynamic_slice_in_dim(dv_all, first_row, value_part.shape[0], 0)
        dv_all = lax.dynamic_update_slice_in_dim(dv_all, old_values + value_part, first_row, 0)
        return (dq_acc + query_part, dk_all, dv_all)

    dq_sum, dk_all, dv_all = over_blocks(
        grads_step_rows,
        grads_initial,
        (
            lax.all_gather(key_rows, "ctx", axis=1, tiled=True)[0],
            lax.all_gather(value_rows, "ctx", axis=1, tiled=True)[0],
        ),
    )
    dk_mine, dv_mine = (
        lax.psum_scatter(dk_all, "ctx", scatter_dimension=0, tiled=True),
        lax.psum_scatter(dv_all, "ctx", scatter_dimension=0, tiled=True),
    )
    query_grad = (dq_sum * factor).astype(jnp.bfloat16).reshape(1, local_rows, QH * HD)
    key_grad = (dk_mine * factor).astype(jnp.bfloat16).reshape(1, local_rows, KVH * HD)
    value_grad = (dv_mine * factor).astype(jnp.bfloat16).reshape(1, local_rows, KVH * HD)
    return (query_grad, key_grad, value_grad)


def solution(mesh):
    in_specs = (
        P("grp", "ctx", None),
        P("grp", "ctx", None),
        P("grp", "ctx", None),
        P("grp", "ctx", None),
        P("grp", "ctx", None),
        P("grp", "ctx"),
        P("grp", None),
        P("grp", None),
    )
    out_specs = (P("grp", "ctx", None), P("grp", "ctx", None), P("grp", "ctx", None))
    return jax.shard_map(shards, mesh=mesh, in_specs=in_specs, out_specs=out_specs, check_vma=False)
```

profile of v0, /device:TPU:8, one launch (start us, length us, event | category | flops | bytes accessed | tf_op | source)
XLA Modules:
  0.0 345.4 jit_solution(4692239312249407797)
XLA Ops:
  8.4 1.3 reduce.7
  11.4 3.4 scatter_fusion
  14.8 6.3 %all-to-all-start = ((bf16[16,8,4096]{2,1,0:T(8,128)(2,1)}), bf16[16,8,4096]{2,1,0:T(8,128)(2,1)S(1)}, u32[]{:S(2)}, u32[]{:S(2)}) async-start(bf16[16,8,4096]{2,1,0:T(8,128)(2,1)} %scatter_fusion), calls=%async_computation | async-start | bytes 2097152 | tf_op jit(solution)/shard_map/all_to_all | solution.py:125
  22.6 1.4 bitcast_multiply_fusion
  25.0 2.9 scatter_fusion.1
  28.0 20.7 %all-to-all-done = bf16[16,8,4096]{2,1,0:T(8,128)(2,1)S(1)} async-done(((bf16[16,8,4096]{2,1,0:T(8,128)(2,1)}), bf16[16,8,4096]{2,1,0:T(8,128)(2,1)S(1)}, u32[]{:S(2)}, u32[]{:S(2)}) %all-to-all-start) | async-done | bytes 1048608 | tf_op jit(solution)/shard_map/all_to_all | solution.py:125
  48.7 6.5 %all-to-all-start.1 = ((bf16[16,8,4096]{2,1,0:T(8,128)(2,1)}), bf16[16,8,4096]{2,1,0:T(8,128)(2,1)}, u32[]{:S(2)}, u32[]{:S(2)}) async-start(bf16[16,8,4096]{2,1,0:T(8,128)(2,1)} %scatter_fusion.1), calls=%async_computation.1 | async-start | bytes 2097152 | tf_op jit(solution)/shard_map/all_to_all | solution.py:126
  56.1 2.5 sort.17
  60.7 3.4 scatter_fusion.2
  64.3 13.2 %all-gather.3.cloned.1.call-done = bf16[1,1024,512]{2,1,0:T(8,128)(2,1)} async-done(((bf16[1,128,512]{2,1,0:T(8,128)(2,1)}), bf16[1,1024,512]{2,1,0:T(8,128)(2,1)}) %all-gather.3.cloned.1.call-update) | async-done | bytes 1048592 | tf_op jit(solution)/shard_map/all_gather | solution.py:187
  77.5 1.5 copy.59
  79.6 6.6 %all-to-all-done.1 = bf16[16,8,4096]{2,1,0:T(8,128)(2,1)} async-done(((bf16[16,8,4096]{2,1,0:T(8,128)(2,1)}), bf16[16,8,4096]{2,1,0:T(8,128)(2,1)}, u32[]{:S(2)}, u32[]{:S(2)}) %all-to-all-start.1) | async-done | bytes 1048608 | tf_op jit(solution)/shard_map/all_to_all | solution.py:126
  86.2 7.0 %all-to-all-start.2 = ((bf16[16,8,4096]{2,1,0:T(8,128)(2,1)}), bf16[16,8,4096]{2,1,0:T(8,128)(2,1)}, u32[]{:S(2)}, u32[]{:S(2)}) async-start(bf16[16,8,4096]{2,1,0:T(8,128)(2,1)} %scatter_fusion.2), calls=%async_computation.2 | async-start | bytes 2097152 | tf_op jit(solution)/shard_map/all_to_all | solution.py:127
  93.2 1.8 gather_fusion.2
  96.9 10.8 %while.28 = (s32[]{:T(128)}, f32[4,8,128]{2,1,0:T(8,128)S(1)}, f32[4,8,128]{2,1,0:T(8,128)S(1)}, s32[2]{0:T(128)S(1)}, s32[12]{0:T(128)S(1)}, /*index=5*/s32[128...) while((s32[]{:T(128)}, f32[4,8,128]{2,1,0:T(8,128)S(1)}, ...), condition=%wide.region_9.11_spmd.clone, body=%wide.region_5.10_spmd.clone.sunk | while | flops 553883776 | bytes 19821336 | solution.py:48
  98.7 1.5 fusion.62
  100.2 2.1 select_reduce_fusion.2
  104.1 1.4 fusion.62
  105.6 2.1 select_reduce_fusion.2
  107.7 1.4 copy.83
  109.2 1.4 copy.62
  110.6 12.3 %all-to-all-done.2 = bf16[16,8,4096]{2,1,0:T(8,128)(2,1)} async-done(((bf16[16,8,4096]{2,1,0:T(8,128)(2,1)}), bf16[16,8,4096]{2,1,0:T(8,128)(2,1)}, u32[]{:S(2)}, u32[]{:S(2)}) %all-to-all-start.2) | async-done | bytes 1048608 | tf_op jit(solution)/shard_map/all_to_all | solution.py:127
  122.9 2.8 gather_fusion.3
  125.7 1.7 multiply_bitcast_fusion
  127.4 1.7 copy.84
  129.1 2.2 reduce_sum.65
  131.6 1.5 broadcast.160.clone
  133.1 1.4 broadcast.160
  134.5 59.4 %while.29 = (s32[]{:T(128)}, f32[128,4,8,128]{0,3,2,1:T(8,128)}, f32[1024,4,128]{2,0,1:T(8,128)}, f32[1024,4,128]{2,0,1:T(8,128)}, bf16[2,512,512]{1,2,0:T(8,128...) while((s32[]{:T(128)}, f32[128,4,8,128]{0,3,2,1:T(8,128)}, ...), condition=%wide.region_15.17_spmd.clone, body=%wide.region_13.16_spmd.clone.sunk | while | flops 2713405440 | bytes 80475096 | solution.py:48
  140.1 1.3 fusion.74
  141.8 3.1 fusion.77
  144.9 3.5 %fusion.75 = bf16[4,8,128,512]{2,3,1,0:T(8,128)(2,1)S(1)} fusion(f32[4,512,128,8]{2,1,3,0:T(8,128)S(1)} %fusion.74, f32[4,8,128]{2,1,0:T(8,128)S(1)} %bitcast.176, f32[4,8,128]{2,1,0:T(8,128)S(1)} %get-tuple-element.587, pred[128,512]{0,1:T(8,128)(4,1)S(1)} %compare_and_fusion.6, bf16[512,4,128,1]{0,2,3,1:T(8,128)(2,1)S(1)} %bitcast.164, ...), kind=kOutput, calls=%fused_computation.23.clone.1 | convolution fusion | flops 553648128 | bytes 14254080 | tf_op jit(solution)/shard_map/while/body/eval_jaxpr/rgsd,ngd->gsrn/dot_general | solution.py:72
  148.5 1.3 fusion.76
  149.8 2.3 bitcast_add_fusion.2
  152.0 5.9 %dynamic_update_slice.10 = f32[1024,4,128]{2,0,1:T(8,128)} dynamic-update-slice(f32[1024,4,128]{2,0,1:T(8,128)} %get-tuple-element.562, f32[512,4,128]{2,0,1:T(8,128)S(1)} %fusion.76, s32[]{:T(128)S(6)} %select_n.158, s32[]{:T(128)} %constant.75.clone.1..sunk.1, s32[]{:T(128)} %constant.75.clone.1..sunk.1) | dynamic-update-slice | bytes 2097156 | tf_op jit(solution)/shard_map/while/body/eval_jaxpr/dynamic_update_slice | solution.py:178
  157.9 6.2 %dynamic_update_slice.11 = f32[1024,4,128]{2,0,1:T(8,128)} dynamic-update-slice(f32[1024,4,128]{2,0,1:T(8,128)} %get-tuple-element.563, f32[512,4,128]{2,0,1:T(8,128)} %fusion.77, s32[]{:T(128)S(6)} %select_n.158, s32[]{:T(128)} %constant.75.clone.1..sunk.1, s32[]{:T(128)} %constant.75.clone.1..sunk.1) | dynamic-update-slice | bytes 2097156 | tf_op jit(solution)/shard_map/while/body/eval_jaxpr/dynamic_update_slice | solution.py:180
  169.7 1.3 fusion.74
  171.4 3.1 fusion.77
  174.5 3.5 %fusion.75 = bf16[4,8,128,512]{2,3,1,0:T(8,128)(2,1)S(1)} fusion(f32[4,512,128,8]{2,1,3,0:T(8,128)S(1)} %fusion.74, f32[4,8,128]{2,1,0:T(8,128)S(1)} %bitcast.176, f32[4,8,128]{2,1,0:T(8,128)S(1)} %get-tuple-element.587, pred[128,512]{0,1:T(8,128)(4,1)S(1)} %compare_and_fusion.6, bf16[512,4,128,1]{0,2,3,1:T(8,128)(2,1)S(1)} %bitcast.164, ...), kind=kOutput, calls=%fused_computation.23.clone.1 | convolution fusion | flops 553648128 | bytes 14254080 | tf_op jit(solution)/shard_map/while/body/eval_jaxpr/rgsd,ngd->gsrn/dot_general | solution.py:72
  178.1 1.3 fusion.76
  179.4 3.9 %bitcast_add_fusion.2 = f32[128,4,8,128]{0,3,2,1:T(8,128)} fusion(f32[128,4,8,128]{0,3,2,1:T(8,128)} %get-tuple-element.561, bf16[512,4,128,1]{0,2,3,1:T(8,128)(2,1)S(1)} %bitcast.162, bf16[4,8,128,512]{2,3,1,0:T(8,128)(2,1)S(1)} %fusion.75, pred[]{:T(512)S(6)} %compare.25), kind=kOutput, calls=%fused_computation.31.clone.1 | convolution fusion | flops 537919488 | bytes 8912897 | tf_op jit(solution)/shard_map/while/body/eval_jaxpr/gsrn,ngd->rgsd/dot_general | solution.py:74
  183.2 5.2 %dynamic_update_slice.10 = f32[1024,4,128]{2,0,1:T(8,128)} dynamic-update-slice(f32[1024,4,128]{2,0,1:T(8,128)} %get-tuple-element.562, f32[512,4,128]{2,0,1:T(8,128)S(1)} %fusion.76, s32[]{:T(128)S(6)} %select_n.158, s32[]{:T(128)} %constant.75.clone.1..sunk.1, s32[]{:T(128)} %constant.75.clone.1..sunk.1) | dynamic-update-slice | bytes 2097156 | tf_op jit(solution)/shard_map/while/body/eval_jaxpr/dynamic_update_slice | solution.py:178
  188.4 5.5 %dynamic_update_slice.11 = f32[1024,4,128]{2,0,1:T(8,128)} dynamic-update-slice(f32[1024,4,128]{2,0,1:T(8,128)} %get-tuple-element.563, f32[512,4,128]{2,0,1:T(8,128)} %fusion.77, s32[]{:T(128)S(6)} %select_n.158, s32[]{:T(128)} %constant.75.clone.1..sunk.1, s32[]{:T(128)} %constant.75.clone.1..sunk.1) | dynamic-update-slice | bytes 2097156 | tf_op jit(solution)/shard_map/while/body/eval_jaxpr/dynamic_update_slice | solution.py:180
  195.1 46.1 %psum.7 = f32[]{:T(128)} all-reduce(f32[]{:T(128)} %convert_reduce_fusion.4), channel_id=1, replica_groups=mesh['grp'=4,'ctx'=8] {'grp','ctx'}, use_global_device_ids=true, to_apply=%region_17.19 | all-reduce | flops 1 | bytes 8 | tf_op jit(solution)/shard_map/psum | solution.py:99
  241.9 1.9 multiply_convert_fusion
  243.8 1.3 copy.74
  245.1 20.5 %reduce-scatter.5.cloned.1.call-done = f32[128,4,128]{2,0,1:T(8,128)} async-done(((f32[1024,4,128]{2,0,1:T(8,128)}), f32[128,4,128]{2,0,1:T(8,128)}) %reduce-scatter.5.cloned.1.call-update) | async-done | bytes 262160 | tf_op jit(solution)/shard_map/reduce_scatter | solution.py:193
  265.6 70.6 %reduce-scatter.3.cloned.1.call-done = f32[128,4,128]{2,0,1:T(8,128)} async-done(((f32[1024,4,128]{2,0,1:T(8,128)}), f32[128,4,128]{2,0,1:T(8,128)}) %reduce-scatter.3.cloned.1.call-update) | async-done | bytes 262160 | tf_op jit(solution)/shard_map/reduce_scatter | solution.py:192
  (107 shorter events, 24.2 us)
Async XLA Ops:
  7.2 48.9 %copy-start.4 = (s32[1,128]{1,0:T(1,128)S(1)}, s32[1,128]{1,0:T(1,128)}, u32[]{:S(2)}) copy-start(s32[1,128]{1,0:T(1,128)} %param.21) | copy-start | bytes 1540
  7.2 48.7 %copy-start.3 = (s32[1,12]{1,0:T(1,128)S(1)}, s32[1,12]{1,0:T(1,128)}, u32[]{:S(2)}) copy-start(s32[1,12]{1,0:T(1,128)} %param.20) | copy-start | bytes 148
  14.8 33.9 %all-to-all-start = ((bf16[16,8,4096]{2,1,0:T(8,128)(2,1)}), bf16[16,8,4096]{2,1,0:T(8,128)(2,1)S(1)}, u32[]{:S(2)}, u32[]{:S(2)}) async-start(bf16[16,8,4096]{2,1,0:T(8,128)(2,1)} %scatter_fusion), calls=%async_computation | async-start | bytes 2097152 | tf_op jit(solution)/shard_map/all_to_all | solution.py:125
  21.1 56.4 %all-gather.3.cloned.1.call-start = ((), (), s32[]{:S(2)}) async-start(), calls=%async_computation.5 | async-start | bytes 1179648 | tf_op jit(solution)/shard_map/all_gather | solution.py:187
  48.7 37.5 %all-to-all-start.1 = ((bf16[16,8,4096]{2,1,0:T(8,128)(2,1)}), bf16[16,8,4096]{2,1,0:T(8,128)(2,1)}, u32[]{:S(2)}, u32[]{:S(2)}) async-start(bf16[16,8,4096]{2,1,0:T(8,128)(2,1)} %scatter_fusion.1), calls=%async_computation.1 | async-start | bytes 2097152 | tf_op jit(solution)/shard_map/all_to_all | solution.py:126
  55.1 76.5 %all-gather.5.cloned.1.call-start = ((), (), s32[]{:S(2)}) async-start(), calls=%async_computation.6 | async-start | bytes 1179648 | tf_op jit(solution)/shard_map/all_gather | solution.py:188
  86.2 36.7 %all-to-all-start.2 = ((bf16[16,8,4096]{2,1,0:T(8,128)(2,1)}), bf16[16,8,4096]{2,1,0:T(8,128)(2,1)}, u32[]{:S(2)}, u32[]{:S(2)}) async-start(bf16[16,8,4096]{2,1,0:T(8,128)(2,1)} %scatter_fusion.2), calls=%async_computation.2 | async-start | bytes 2097152 | tf_op jit(solution)/shard_map/all_to_all | solution.py:127
  93.2 172.4 %reduce-scatter.5.cloned.1.call-start = ((), (), s32[]{:S(2)}) async-start(), calls=%async_computation.8 | async-start | bytes 2359296 | tf_op jit(solution)/shard_map/reduce_scatter | solution.py:193
  134.5 60.0 %copy-start.5 = (s32[1,128]{1,0:T(1,128)S(1)}, s32[1,128]{1,0:T(1,128)}, u32[]{:S(2)}) copy-start(s32[1,128]{1,0:T(1,128)} %param.19) | copy-start | bytes 1540
  140.0 1.6 copy-start.1
  140.0 1.8 copy-start.2
  144.9 3.6 %copy-start = (f32[1024,4,128]{2,0,1:T(8,128)S(1)}, f32[1024,4,128]{2,0,1:T(8,128)}, u32[]{:S(2)}) copy-start(f32[1024,4,128]{2,0,1:T(8,128)} %get-tuple-element.562) | copy-start | bytes 6291460 | tf_op jit(solution)/shard_map/while
  169.6 1.6 copy-start.1
  169.6 1.8 copy-start.2
  174.5 3.6 %copy-start = (f32[1024,4,128]{2,0,1:T(8,128)S(1)}, f32[1024,4,128]{2,0,1:T(8,128)}, u32[]{:S(2)}) copy-start(f32[1024,4,128]{2,0,1:T(8,128)} %get-tuple-element.562) | copy-start | bytes 6291460 | tf_op jit(solution)/shard_map/while
  194.0 142.2 %reduce-scatter.3.cloned.1.call-start = ((), (), s32[]{:S(2)}) async-start(), calls=%async_computation.7 | async-start | bytes 2359296 | tf_op jit(solution)/shard_map/reduce_scatter | solution.py:192
Sparse Core Ops, SparseCore 0:
  24.0 53.4 all-gather.2
  79.6 51.9 all-gather.4
  194.1 71.4 reduce-scatter.4
  269.0 67.1 reduce-scatter.2
where the time goes:
time: 349 us; the launch traced here: 345 us
  waiting for transfers between devices  146 us (42%)
  local copies, waits for them, and re-layouts  62.6 us (18%)
  blocking collectives  46.1 us (13%)
  matrix products  27.4 us (8%)
  other arithmetic  21.9 us (6%)
  starting transfers between devices  19.8 us (6%)
  between operations  14.6 us (4%)
  loops' own time  6.75 us (2%)
    reduce_scatter x1, waiting for transfers between devices, shards(): lax.psum_scatter(dk_all, 'ctx', scatter_dimension=0, tiled=True)  70.6 us
    psum x1, blocking collectives, shards(): total_counted = lax.psum(counted, ('grp', 'ctx'))  46.1 us
    all_to_all x1, waiting for transfers between devices, shards(): lax.all_to_all(pack_rows(query_rows[0]), 'ctx', split_axis=0, concat_axis...  20.7 us
    reduce_scatter x1, waiting for transfers between devices, shards(): lax.psum_scatter(dv_all, 'ctx', scatter_dimension=0, tiled=True)  20.5 us
    all_gather x1, waiting for transfers between devices, shards(): lax.all_gather(key_rows, 'ctx', axis=1, tiled=True)[0]  13.2 us
    all_to_all x1, waiting for transfers between devices, shards(): lax.all_to_all(pack_rows(output_rows[0]), 'ctx', split_axis=0, concat_axi...  12.3 us
    dynamic_update_slice x2, local copies, waits for them, and re-layouts, grads_step_rows(): lax.dynamic_update_slice_in_dim(dv_all, old_values + value_part, first_ro...  11.7 us
    dynamic_update_slice x2, local copies, waits for them, and re-layouts, grads_step_rows(): lax.dynamic_update_slice_in_dim(dk_all, old_keys + key_part, first_row, 0)  11.1 us
  transfers between devices with their start and end apart: 7, of which 7 were waited for; matrix products, arithmetic and copies ran while one was open for 13% of the time, Pallas kernels for 0%

commit v1 on v0

v1 whole, which is shorter than its diff:
```python
import functools
import math

import jax
import jax.numpy as jnp
from jax import lax
from jax.experimental import pallas as pl
from jax.experimental.pallas import tpu as pltpu
from jax.sharding import PartitionSpec as P

HD = 128
QH = 32
KVH = 4
SPAN = 8
GROUP = QH // KVH
NEGATIVE = -1e30
MESH = pl.DeviceIdType.MESH


def dot(a, b, ca, cb):
    return lax.dot_general(a, b, (((ca,), (cb,)), ((), ())), preferred_element_type=jnp.float32)


def kernel(
    n, grps, halo, pair_rows,
    q_ref, k_ref, v_ref, o_ref, g_ref, mask_ref, docs_ref, plan_ref,
    dq_ref, dk_ref, dv_ref,
    kvwin, part_send, part_recv, part_own, dq_send, dq_recv, cnt_ctx, cnt_grp, bias_ref,
    kv_ss, kv_rs, pt_ss, pt_rs, dq_ss, dq_rs, c1_ss, c1_rs, c2_ss, c2_rs,
):
    me = lax.axis_index("ctx")
    my_grp = lax.axis_index("grp")
    rows = q_ref.shape[1]
    spans = plan_ref.shape[1]
    per_device = rows // SPAN
    slots = halo + 1
    window = slots * rows
    width = GROUP * HD
    peers = [lax.rem(me + step, n) for step in range(1, n)]
    grp_peers = [lax.rem(my_grp + step, grps) for step in range(1, grps)]

    barrier = pltpu.get_barrier_semaphore()
    for peer in peers:
        pl.semaphore_signal(barrier, inc=1, device_id={"ctx": peer}, device_id_type=MESH)
    for peer in grp_peers:
        pl.semaphore_signal(barrier, inc=1, device_id={"grp": peer}, device_id_type=MESH)

    for g in range(KVH):
        kvwin[g, 0, halo] = k_ref[0, :, g * HD:(g + 1) * HD]
        kvwin[g, 1, halo] = v_ref[0, :, g * HD:(g + 1) * HD]
    mask_f = mask_ref[...].astype(jnp.float32)
    cnt_ctx[me] = jnp.broadcast_to(jnp.sum(mask_f, axis=1, keepdims=True), (8, 128))

    pl.semaphore_wait(barrier, n - 1 + grps - 1)

    def kv_copy(g, s, target):
        return pltpu.make_async_remote_copy(
            src_ref=kvwin.at[g, :, halo], dst_ref=kvwin.at[g, :, halo - s],
            send_sem=kv_ss.at[g, s - 1], recv_sem=kv_rs.at[g, s - 1],
            device_id={"ctx": target}, device_id_type=MESH)

    def part_copy(g, s, target):
        return pltpu.make_async_remote_copy(
            src_ref=part_send.at[g, s - 1], dst_ref=part_recv.at[g, s - 1],
            send_sem=pt_ss.at[g, s - 1], recv_sem=pt_rs.at[g, s - 1],
            device_id={"ctx": target}, device_id_type=MESH)

    def dq_out(g, peer):
        return pltpu.make_async_remote_copy(
            src_ref=dq_send.at[g, peer], dst_ref=dq_recv.at[g, me],
            send_sem=dq_ss.at[g, peer], recv_sem=dq_rs.at[g, me],
            device_id={"ctx": peer}, device_id_type=MESH)

    def dq_in(g, peer):
        return pltpu.make_async_remote_copy(
            src_ref=dq_send.at[g, peer], dst_ref=dq_recv.at[g, peer],
            send_sem=dq_ss.at[g, peer], recv_sem=dq_rs.at[g, peer],
            device_id={"ctx": peer}, device_id_type=MESH)

    def count_copy(buffer, ss, rs, axis, own, slot, peer):
        return pltpu.make_async_remote_copy(
            src_ref=buffer.at[own], dst_ref=buffer.at[slot],
            send_sem=ss.at[peer], recv_sem=rs.at[slot],
            device_id={axis: peer}, device_id_type=MESH)

    for peer in peers:
        count_copy(cnt_ctx, c1_ss, c1_rs, "ctx", me, me, peer).start()
    for g in range(KVH):
        for s in range(1, halo + 1):
            @pl.when(me + s < n)
            def _():
                kv_copy(g, s, me + s).start()

    plan_f = plan_ref[...].astype(jnp.float32)
    plan_b = jnp.broadcast_to(plan_f, (spans, spans))
    plan_t = jnp.transpose(plan_b)
    dest_b = jnp.floor(plan_b * (1.0 / per_device))
    dest_t = jnp.floor(plan_t * (1.0 / per_device))
    row_id = lax.broadcasted_iota(jnp.int32, (spans, spans), 0)
    col_id = lax.broadcasted_iota(jnp.int32, (spans, spans), 1)
    earlier = (dest_b == dest_t) & (row_id // per_device == col_id // per_device) & (col_id < row_id)
    rank_t = jnp.sum(jnp.where(earlier, 1.0, 0.0), axis=1, keepdims=True)
    span_id = lax.broadcasted_iota(jnp.int32, (spans, rows), 0)
    tok_id = lax.broadcasted_iota(jnp.int32, (spans, rows), 1)
    dest_c = dest_t[:, :1]
    plan_c = plan_t[:, :1]
    send_c = dest_c * float(pair_rows) + rank_t * float(SPAN)
    origin = (lax.broadcasted_iota(jnp.int32, (spans, 1), 0) // per_device).astype(jnp.float32)
    recv_c = origin * float(pair_rows) + rank_t * float(SPAN)
    tok = lax.broadcasted_iota(jnp.int32, (1, rows), 1)
    within = lax.rem(tok, SPAN).astype(jnp.float32)
    own_span = span_id == me * per_device + tok_id // SPAN
    send_row = jnp.sum(jnp.where(own_span, send_c, 0.0), axis=0, keepdims=True) + within
    slot_f = (me * per_device + tok_id // SPAN).astype(jnp.float32)
    recv_row = jnp.sum(jnp.where(plan_c == slot_f, recv_c, 0.0), axis=0, keepdims=True) + within
    buffer_id = lax.broadcasted_iota(jnp.int32, (n * pair_rows, rows), 0).astype(jnp.float32)
    pack = jnp.where(buffer_id == send_row, 1.0, 0.0).astype(jnp.bfloat16)
    unpack = jnp.transpose(jnp.where(buffer_id == recv_row, 1.0, 0.0)).astype(jnp.bfloat16)

    query_pos = me * rows + tok
    start = jnp.zeros_like(query_pos)
    end = jnp.int32(0)
    for m in range(docs_ref.shape[1]):
        end = end + docs_ref[0, m]
        start = jnp.where(query_pos >= end, end, start)
    key_pos = (me - halo) * rows + lax.broadcasted_iota(jnp.int32, (window, rows), 0)
    bias_ref[...] = jnp.where((key_pos >= start) & (key_pos <= query_pos), 0.0, NEGATIVE)
    mask_col = jnp.transpose(jnp.broadcast_to(mask_f, (HD, rows))).astype(jnp.bfloat16)

    for peer in peers:
        count_copy(cnt_ctx, c1_ss, c1_rs, "ctx", me, peer, peer).wait_recv()
    cnt_grp[my_grp] = jnp.sum(cnt_ctx[...], axis=0)
    for peer in grp_peers:
        count_copy(cnt_grp, c2_ss, c2_rs, "grp", my_grp, my_grp, peer).start()

    scale_value = HD ** (-0.5)
    exp_scale = scale_value * math.log2(math.e)
    ones = jnp.ones((8, 2 * HD), jnp.bfloat16)
    factor = None
    for g in range(KVH):
        for s in range(1, halo + 1):
            @pl.when(me >= s)
            def _():
                kv_copy(g, s, me).wait_recv()

            @pl.when(me < s)
            def _():
                kvwin[g, :, halo - s] = jnp.zeros((2, rows, HD), jnp.bfloat16)
        keys = kvwin[g, 0].reshape(window, HD)
        values = kvwin[g, 1].reshape(window, HD)
        keys_t = jnp.transpose(keys)
        dk_sum = jnp.zeros((window, HD), jnp.float32)
        dv_sum = jnp.zeros((window, HD), jnp.float32)
        for pair in range(GROUP // 2):
            columns = [slice(h * HD, (h + 1) * HD) for h in (g * GROUP + 2 * pair, g * GROUP + 2 * pair + 1)]
            queries = jnp.concatenate([q_ref[0, :, c] for c in columns], axis=0)
            grads = jnp.concatenate([g_ref[0, :, c] * mask_col for c in columns], axis=0)
            outputs = jnp.concatenate([o_ref[0, :, c] for c in columns], axis=0)
            product = grads.astype(jnp.float32) * outputs.astype(jnp.float32)
            high = product.astype(jnp.bfloat16)
            low = (product - high.astype(jnp.float32)).astype(jnp.bfloat16)
            delta = dot(ones, jnp.concatenate([high, low], axis=1), 1, 1)[:1]
            bias = bias_ref[...]
            scores = dot(keys, queries, 1, 1) * exp_scale + jnp.concatenate([bias, bias], axis=1)
            weights = jnp.exp2(scores - jnp.max(scores, axis=0, keepdims=True))
            probs = weights * (1.0 / jnp.sum(weights, axis=0, keepdims=True))
            dprobs = dot(values, grads, 1, 1)
            dscores = (probs * (dprobs - delta) * scale_value).astype(jnp.bfloat16)
            dq_t = dot(keys_t, dscores, 1, 0)
            if factor is None:
                for peer in grp_peers:
                    count_copy(cnt_grp, c2_ss, c2_rs, "grp", my_grp, peer, peer).wait_recv()
                counted = jnp.sum(cnt_grp[...], axis=0)[:1, :]
                factor = float(grps * n * rows) / jnp.maximum(counted, 1.0)
            dq_half = (dq_t * factor[:, :1]).astype(jnp.bfloat16)
            for i in range(2):
                packed = dot(pack, dq_half[:, i * rows:(i + 1) * rows], 1, 1).astype(jnp.bfloat16)
                local = (2 * pair + i) * HD
                dq_send[g, :, :, local:local + HD] = packed.reshape(n, pair_rows, HD)
            dk_sum += dot(dscores, queries, 1, 0)
            dv_sum += dot(probs.astype(jnp.bfloat16), grads, 1, 0)
        for peer in peers:
            dq_out(g, peer).start()
        dq_recv[g, me] = dq_send[g, me]
        for s in range(1, halo + 1):
            at = slice((halo - s) * rows, (halo - s + 1) * rows)
            part_send[g, s - 1, 0] = dk_sum[at].astype(jnp.bfloat16)
            part_send[g, s - 1, 1] = dv_sum[at].astype(jnp.bfloat16)

            @pl.when(me >= s)
            def _():
                part_copy(g, s, me - s).start()
        part_own[g, 0] = dk_sum[halo * rows:]
        part_own[g, 1] = dv_sum[halo * rows:]

    for g in range(KVH):
        for s in range(1, halo + 1):
            @pl.when(me + s < n)
            def _():
                part_copy(g, s, me).wait_recv()

            @pl.when(me + s >= n)
            def _():
                part_recv[g, s - 1] = jnp.zeros((2, rows, HD), jnp.bfloat16)
        total = part_own[g]
        for s in range(1, halo + 1):
            total += part_recv[g, s - 1].astype(jnp.float32)
        total = (total * factor[:, :1]).astype(jnp.bfloat16)
        dk_ref[0, :, g * HD:(g + 1) * HD] = total[0]
        dv_ref[0, :, g * HD:(g + 1) * HD] = total[1]
        for peer in peers:
            dq_in(g, peer).wait_recv()
        dq_ref[0, :, g * width:(g + 1) * width] = dot(
            unpack, dq_recv[g].reshape(n * pair_rows, width), 1, 0).astype(jnp.bfloat16)

    for peer in peers:
        count_copy(cnt_ctx, c1_ss, c1_rs, "ctx", me, me, peer).wait_send()
    for peer in grp_peers:
        count_copy(cnt_grp, c2_ss, c2_rs, "grp", my_grp, my_grp, peer).wait_send()
    for g in range(KVH):
        for s in range(1, halo + 1):
            @pl.when(me + s < n)
            def _():
                kv_copy(g, s, me + s).wait_send()

            @pl.when(me >= s)
            def _():
                part_copy(g, s, me - s).wait_send()
        for peer in peers:
            dq_out(g, peer).wait_send()


def solution(mesh):
    n, grps = mesh.shape["ctx"], mesh.shape["grp"]

    def shards(*args):
        rows = args[0].shape[1]
        halo = min(n - 1, -(-(n * rows // 4 - 1) // rows))
        slot_count = -(-(rows // SPAN) // n)
        pair_rows = -(-slot_count * SPAN // 16) * 16
        vmem = pl.BlockSpec(memory_space=pltpu.VMEM)
        smem = pl.BlockSpec(memory_space=pltpu.SMEM)
        dma = pltpu.SemaphoreType.DMA
        bf16, f32 = jnp.bfloat16, jnp.float32
        return pl.pallas_call(
            functools.partial(kernel, n, grps, halo, pair_rows),
            out_shape=[
                jax.ShapeDtypeStruct((1, rows, QH * HD), bf16),
                jax.ShapeDtypeStruct((1, rows, KVH * HD), bf16),
                jax.ShapeDtypeStruct((1, rows, KVH * HD), bf16),
            ],
            in_specs=[vmem] * 6 + [smem, vmem],
            out_specs=[vmem] * 3,
            scratch_shapes=[
                pltpu.VMEM((KVH, 2, halo + 1, rows, HD), bf16),
                pltpu.VMEM((KVH, halo, 2, rows, HD), bf16),
                pltpu.VMEM((KVH, halo, 2, rows, HD), bf16),
                pltpu.VMEM((KVH, 2, rows, HD), f32),
                pltpu.VMEM((KVH, n, pair_rows, GROUP * HD), bf16),
                pltpu.VMEM((KVH, n, pair_rows, GROUP * HD), bf16),
                pltpu.VMEM((n, 8, 128), f32),
                pltpu.VMEM((grps, 8, 128), f32),
                pltpu.VMEM(((halo + 1) * rows, rows), f32),
                dma((KVH, halo)), dma((KVH, halo)),
                dma((KVH, halo)), dma((KVH, halo)),
                dma((KVH, n)), dma((KVH, n)),
                dma((n,)), dma((n,)), dma((grps,)), dma((grps,)),
            ],
            compiler_params=pltpu.CompilerParams(
                collective_id=0, has_side_effects=True, vmem_limit_bytes=48 * 1024 * 1024),
            cost_estimate=pl.CostEstimate(
                flops=10 * (halo + 1) * rows * rows * QH * HD, bytes_accessed=9 * rows * QH * HD,
                transcendentals=(halo + 1) * rows * rows * QH),
        )(*args)

    in_specs = (
        P("grp", "ctx", None),
        P("grp", "ctx", None),
        P("grp", "ctx", None),
        P("grp", "ctx", None),
        P("grp", "ctx", None),
        P("grp", "ctx"),
        P("grp", None),
        P("grp", None),
    )
    out_specs = (P("grp", "ctx", None), P("grp", "ctx", None), P("grp", "ctx", None))
    return jax.shard_map(shards, mesh=mesh, in_specs=in_specs, out_specs=out_specs, check_vma=False)
```

time: 349 us -> 61.3 us (0.18)
  waiting for transfers between devices: 146 us -> 0 us
  local copies, waits for them, and re-layouts: 62.6 us -> 9.72 us
  Pallas kernels: 0 us -> 50.6 us
  blocking collectives: 46.1 us -> 0 us
  matrix products: 27.4 us -> 0 us
  other arithmetic: 21.9 us -> 0 us
  starting transfers between devices: 19.8 us -> 0 us
  between operations: 14.6 us -> 0.66 us
  loops' own time: 6.75 us -> 0 us
    reduce_scatter x2 -> x0, waiting for transfers between devices: 91.1 us -> none  [the longest x1 70.6 us: shards(): lax.psum_scatter(dk_all, 'ctx', scatter_dimension=0, tiled=True)]
    pallas_call x0 -> x1, Pallas kernels: none -> 50.6 us  [shards(): pl.pallas_call(functools.partial(kernel, n, grps, halo, pair_rows), out_s...]
    psum x1 -> x0, blocking collectives: 46.1 us -> none  [shards(): total_counted = lax.psum(counted, ('grp', 'ctx'))]
    all_to_all x3 -> x0, waiting for transfers between devices: 39.6 us -> none  [the longest x1 20.7 us: shards(): lax.all_to_all(pack_rows(query_rows[0]), 'ctx', split_axis=0, concat_axis...]
    dot_general x12 -> x0, matrix products: 27.4 us -> none  [the longest x2 7.08 us: block_grads(): jnp.einsum('rgsd,ngd->gsrn', g_heads, v_heads, preferred_element_type=jnp...]
    dynamic_update_slice x4 -> x0, local copies, waits for them, and re-layouts: 22.8 us -> none  [the longest x2 11.7 us: grads_step_rows(): lax.dynamic_update_slice_in_dim(dv_all, old_values + value_part, first_ro...]
    all_to_all x3 -> x0, starting transfers between devices: 19.8 us -> none  [the longest x1 7.03 us: shards(): lax.all_to_all(pack_rows(output_rows[0]), 'ctx', split_axis=0, concat_axi...]
    all_gather x2 -> x0, waiting for transfers between devices: 13.5 us -> none  [the longest x1 13.2 us: shards(): lax.all_gather(key_rows, 'ctx', axis=1, tiled=True)[0]]
  transfers between devices with their start and end apart: 7 -> 0, of which waited for: 7 -> 0; matrix products, arithmetic and copies ran while one was open for 13% -> 0% of each run, Pallas kernels for 0% -> 0%
where the time goes in v1:
time: 61.3 us; the launch traced here: 61 us
  Pallas kernels  50.6 us (83%)
  local copies, waits for them, and re-layouts  9.72 us (16%)
  between operations  0.66 us (1%)
    pallas_call x1, Pallas kernels, shards(): pl.pallas_call(functools.partial(kernel, n, grps, halo, pair_rows), out_s...  50.6 us
    unnamed x19, local copies, waits for them, and re-layouts  9.72 us

profile of v1, /device:TPU:8, one launch (start us, length us, event | category | flops | bytes accessed | tf_op | source)
XLA Modules:
  0.0 61.0 jit_solution(3332131387323637618)
XLA Ops:
  0.6 0.0 copy-start
  0.6 1.2 %copy-done = bf16[1,128,4096]{2,1,0:T(8,128)(2,1)S(1)} copy-done((bf16[1,128,4096]{2,1,0:T(8,128)(2,1)S(1)}, bf16[1,128,4096]{2,1,0:T(8,128)(2,1)}, u32[]{:S(2)}) %copy-start) | copy-done | bytes 1048600
  1.9 0.0 copy-start.1
  1.9 1.2 %copy-done.1 = bf16[1,128,4096]{2,1,0:T(8,128)(2,1)S(1)} copy-done((bf16[1,128,4096]{2,1,0:T(8,128)(2,1)S(1)}, bf16[1,128,4096]{2,1,0:T(8,128)(2,1)}, u32[]{:S(2)}) %copy-start.1) | copy-done | bytes 1048600
  3.1 0.0 copy-start.2
  3.1 1.2 %copy-done.2 = bf16[1,128,4096]{2,1,0:T(8,128)(2,1)S(1)} copy-done((bf16[1,128,4096]{2,1,0:T(8,128)(2,1)S(1)}, bf16[1,128,4096]{2,1,0:T(8,128)(2,1)}, u32[]{:S(2)}) %copy-start.2) | copy-done | bytes 1048600
  4.3 0.0 copy-start.3
  4.3 0.9 %copy-done.3 = bf16[1,128,512]{2,1,0:T(8,128)(2,1)S(1)} copy-done((bf16[1,128,512]{2,1,0:T(8,128)(2,1)S(1)}, bf16[1,128,512]{2,1,0:T(8,128)(2,1)}, u32[]{:S(2)}) %copy-start.3) | copy-done | bytes 131096
  5.2 0.0 copy-start.4
  5.2 0.9 %copy-done.4 = bf16[1,128,512]{2,1,0:T(8,128)(2,1)S(1)} copy-done((bf16[1,128,512]{2,1,0:T(8,128)(2,1)S(1)}, bf16[1,128,512]{2,1,0:T(8,128)(2,1)}, u32[]{:S(2)}) %copy-start.4) | copy-done | bytes 131096
  6.1 0.0 copy-start.5
  6.1 0.7 %copy-done.5 = s32[1,128]{1,0:T(1,128)S(1)} copy-done((s32[1,128]{1,0:T(1,128)S(1)}, s32[1,128]{1,0:T(1,128)}, u32[]{:S(2)}) %copy-start.5) | copy-done | bytes 536
  6.8 0.0 copy-start.6
  6.8 0.7 %copy-done.6 = s32[1,12]{1,0:T(1,128)S(1)} copy-done((s32[1,12]{1,0:T(1,128)S(1)}, s32[1,12]{1,0:T(1,128)}, u32[]{:S(2)}) %copy-start.6) | copy-done | bytes 72
  7.4 0.0 copy-start.7
  7.4 0.7 %copy-done.7 = s32[1,128]{1,0:T(1,128)S(1)} copy-done((s32[1,128]{1,0:T(1,128)S(1)}, s32[1,128]{1,0:T(1,128)}, u32[]{:S(2)}) %copy-start.7) | copy-done | bytes 536
  8.1 50.6 %shard_map.103 = (bf16[1,128,4096]{2,1,0:T(8,128)(2,1)S(1)}, bf16[1,128,512]{2,1,0:T(8,128)(2,1)S(1)}, bf16[1,128,512]{2,1,0:T(8,128)(2,1)S(1)}) custom-call(bf16[1,128,4096]{2,1,0:T(8,128)(2,1)S(1)} %copy-done, bf16[1,128,512]{2,1,0:T(8,128)(2,1)S(1)} %copy-done.3, bf16[1,128,512]{2,1,0:T(8,128)(2,1)S(1)} %copy-done.4, bf16[1,128,4096]{2,1,0:T(8,128)(2,1)S(1)} %copy-done.1, ...), custom_call_target="tpu_custom_call" | custom-call | flops 2013265920 | bytes 4718592 | tf_op jit(solution)/shard_map/pallas_call | solution.py:245
  58.7 1.0 %copy.14 = bf16[1,128,4096]{2,1,0:T(8,128)(2,1)} copy(bf16[1,128,4096]{2,1,0:T(8,128)(2,1)S(1)} %get-tuple-element.6) | data formatting | bytes 2097152
  59.7 0.7 %copy.15 = bf16[1,128,512]{2,1,0:T(8,128)(2,1)} copy(bf16[1,128,512]{2,1,0:T(8,128)(2,1)S(1)} %get-tuple-element.7) | data formatting | bytes 262144
  60.4 0.7 %copy.16 = bf16[1,128,512]{2,1,0:T(8,128)(2,1)} copy(bf16[1,128,512]{2,1,0:T(8,128)(2,1)S(1)} %get-tuple-element.8) | data formatting | bytes 262144
Async XLA Ops:
  0.6 1.2 %copy-start = (bf16[1,128,4096]{2,1,0:T(8,128)(2,1)S(1)}, bf16[1,128,4096]{2,1,0:T(8,128)(2,1)}, u32[]{:S(2)}) copy-start(bf16[1,128,4096]{2,1,0:T(8,128)(2,1)} %q_ref.1) | copy-start | bytes 3145732
  1.9 1.2 %copy-start.1 = (bf16[1,128,4096]{2,1,0:T(8,128)(2,1)S(1)}, bf16[1,128,4096]{2,1,0:T(8,128)(2,1)}, u32[]{:S(2)}) copy-start(bf16[1,128,4096]{2,1,0:T(8,128)(2,1)} %o_ref.1) | copy-start | bytes 3145732
  3.1 1.2 %copy-start.2 = (bf16[1,128,4096]{2,1,0:T(8,128)(2,1)S(1)}, bf16[1,128,4096]{2,1,0:T(8,128)(2,1)}, u32[]{:S(2)}) copy-start(bf16[1,128,4096]{2,1,0:T(8,128)(2,1)} %g_ref.1) | copy-start | bytes 3145732
  4.3 0.9 %copy-start.3 = (bf16[1,128,512]{2,1,0:T(8,128)(2,1)S(1)}, bf16[1,128,512]{2,1,0:T(8,128)(2,1)}, u32[]{:S(2)}) copy-start(bf16[1,128,512]{2,1,0:T(8,128)(2,1)} %k_ref.1) | copy-start | bytes 393220
  5.2 0.9 %copy-start.4 = (bf16[1,128,512]{2,1,0:T(8,128)(2,1)S(1)}, bf16[1,128,512]{2,1,0:T(8,128)(2,1)}, u32[]{:S(2)}) copy-start(bf16[1,128,512]{2,1,0:T(8,128)(2,1)} %v_ref.1) | copy-start | bytes 393220
  6.1 0.7 %copy-start.5 = (s32[1,128]{1,0:T(1,128)S(1)}, s32[1,128]{1,0:T(1,128)}, u32[]{:S(2)}) copy-start(s32[1,128]{1,0:T(1,128)} %mask_ref.1) | copy-start | bytes 1540
  6.8 0.7 %copy-start.6 = (s32[1,12]{1,0:T(1,128)S(1)}, s32[1,12]{1,0:T(1,128)}, u32[]{:S(2)}) copy-start(s32[1,12]{1,0:T(1,128)} %docs_ref.1) | copy-start | bytes 148
  7.4 0.7 %copy-start.7 = (s32[1,128]{1,0:T(1,128)S(1)}, s32[1,128]{1,0:T(1,128)}, u32[]{:S(2)}) copy-start(s32[1,128]{1,0:T(1,128)} %plan_ref.1) | copy-start | bytes 1540

commit v2 on v1

--- a/solution.py
+++ b/solution.py
@@ -23,21 +23,42 @@
 
 def kernel(
     n, grps, halo, pair_rows,
-    q_ref, k_ref, v_ref, o_ref, g_ref, mask_ref, docs_ref, plan_ref,
+    q_hbm, k_hbm, v_hbm, o_hbm, g_hbm, mask_hbm, docs_hbm, plan_hbm,
     dq_ref, dk_ref, dv_ref,
     kvwin, part_send, part_recv, part_own, dq_send, dq_recv, cnt_ctx, cnt_grp, bias_ref,
+    q_ref, o_ref, g_ref, mask_ref, docs_ref, plan_ref, kv_in, qog_in, small_in,
     kv_ss, kv_rs, pt_ss, pt_rs, dq_ss, dq_rs, c1_ss, c1_rs, c2_ss, c2_rs,
 ):
     me = lax.axis_index("ctx")
     my_grp = lax.axis_index("grp")
-    rows = q_ref.shape[1]
+    rows = q_ref.shape[0]
     spans = plan_ref.shape[1]
     per_device = rows // SPAN
     slots = halo + 1
     window = slots * rows
     width = GROUP * HD
-    peers = [lax.rem(me + step, n) for step in range(1, n)]
+    steps = sorted(range(1, n), key=lambda step: (abs(2 * step - n), step))
+    peers = [lax.rem(me + step, n) for step in steps]
     grp_peers = [lax.rem(my_grp + step, grps) for step in range(1, grps)]
+
+    def fetch(source, target, sem):
+        copy = pltpu.make_async_copy(source, target, sem)
+        copy.start()
+        return copy
+
+    mask_copy = fetch(mask_hbm, mask_ref, small_in.at[0])
+    kv_copies = [
+        [fetch(ref.at[0, :, g * HD:(g + 1) * HD], kvwin.at[g, i, halo], kv_in.at[g, i])
+         for i, ref in enumerate((k_hbm, v_hbm))]
+        for g in range(KVH)
+    ]
+    plan_copy = fetch(plan_hbm, plan_ref, small_in.at[1])
+    docs_copy = fetch(docs_hbm, docs_ref, small_in.at[2])
+    qog_copies = [
+        [fetch(source.at[0, :, g * width:(g + 1) * width], target.at[:, g * width:(g + 1) * width], qog_in.at[g, i])
+         for i, (source, target) in enumerate(((q_hbm, q_ref), (o_hbm, o_ref), (g_hbm, g_ref)))]
+        for g in range(KVH)
+    ]
 
     barrier = pltpu.get_barrier_semaphore()
     for peer in peers:
@@ -45,9 +66,7 @@
     for peer in grp_peers:
         pl.semaphore_signal(barrier, inc=1, device_id={"grp": peer}, device_id_type=MESH)
 
-    for g in range(KVH):
-        kvwin[g, 0, halo] = k_ref[0, :, g * HD:(g + 1) * HD]
-        kvwin[g, 1, halo] = v_ref[0, :, g * HD:(g + 1) * HD]
+    mask_copy.wait()
     mask_f = mask_ref[...].astype(jnp.float32)
     cnt_ctx[me] = jnp.broadcast_to(jnp.sum(mask_f, axis=1, keepdims=True), (8, 128))
 
@@ -86,11 +105,15 @@
     for peer in peers:
         count_copy(cnt_ctx, c1_ss, c1_rs, "ctx", me, me, peer).start()
     for g in range(KVH):
+        for copy in kv_copies[g]:
+            copy.wait()
         for s in range(1, halo + 1):
             @pl.when(me + s < n)
             def _():
                 kv_copy(g, s, me + s).start()
 
+    plan_copy.wait()
+    docs_copy.wait()
     plan_f = plan_ref[...].astype(jnp.float32)
     plan_b = jnp.broadcast_to(plan_f, (spans, spans))
     plan_t = jnp.transpose(plan_b)
@@ -146,6 +169,8 @@
             @pl.when(me < s)
             def _():
                 kvwin[g, :, halo - s] = jnp.zeros((2, rows, HD), jnp.bfloat16)
+        for copy in qog_copies[g]:
+            copy.wait()
         keys = kvwin[g, 0].reshape(window, HD)
         values = kvwin[g, 1].reshape(window, HD)
         keys_t = jnp.transpose(keys)
@@ -153,9 +178,9 @@
         dv_sum = jnp.zeros((window, HD), jnp.float32)
         for pair in range(GROUP // 2):
             columns = [slice(h * HD, (h + 1) * HD) for h in (g * GROUP + 2 * pair, g * GROUP + 2 * pair + 1)]
-            queries = jnp.concatenate([q_ref[0, :, c] for c in columns], axis=0)
-            grads = jnp.concatenate([g_ref[0, :, c] * mask_col for c in columns], axis=0)
-            outputs = jnp.concatenate([o_ref[0, :, c] for c in columns], axis=0)
+            queries = jnp.concatenate([q_ref[:, c] for c in columns], axis=0)
+            grads = jnp.concatenate([g_ref[:, c] * mask_col for c in columns], axis=0)
+            outputs = jnp.concatenate([o_ref[:, c] for c in columns], axis=0)
             product = grads.astype(jnp.float32) * outputs.astype(jnp.float32)
             high = product.astype(jnp.bfloat16)
             low = (product - high.astype(jnp.float32)).astype(jnp.bfloat16)
@@ -239,7 +264,6 @@
         slot_count = -(-(rows // SPAN) // n)
         pair_rows = -(-slot_count * SPAN // 16) * 16
         vmem = pl.BlockSpec(memory_space=pltpu.VMEM)
-        smem = pl.BlockSpec(memory_space=pltpu.SMEM)
         dma = pltpu.SemaphoreType.DMA
         bf16, f32 = jnp.bfloat16, jnp.float32
         return pl.pallas_call(
@@ -249,7 +273,7 @@
                 jax.ShapeDtypeStruct((1, rows, KVH * HD), bf16),
                 jax.ShapeDtypeStruct((1, rows, KVH * HD), bf16),
             ],
-            in_specs=[vmem] * 6 + [smem, vmem],
+            in_specs=[pl.BlockSpec(memory_space=pltpu.HBM)] * 8,
             out_specs=[vmem] * 3,
             scratch_shapes=[
                 pltpu.VMEM((KVH, 2, halo + 1, rows, HD), bf16),
@@ -261,13 +285,20 @@
                 pltpu.VMEM((n, 8, 128), f32),
                 pltpu.VMEM((grps, 8, 128), f32),
                 pltpu.VMEM(((halo + 1) * rows, rows), f32),
+                pltpu.VMEM((rows, QH * HD), bf16),
+                pltpu.VMEM((rows, QH * HD), bf16),
+                pltpu.VMEM((rows, QH * HD), bf16),
+                pltpu.VMEM((1, rows), jnp.int32),
+                pltpu.SMEM(args[6].shape, jnp.int32),
+                pltpu.VMEM(args[7].shape, jnp.int32),
+                dma((KVH, 2)), dma((KVH, 3)), dma((3,)),
                 dma((KVH, halo)), dma((KVH, halo)),
                 dma((KVH, halo)), dma((KVH, halo)),
                 dma((KVH, n)), dma((KVH, n)),
                 dma((n,)), dma((n,)), dma((grps,)), dma((grps,)),
             ],
             compiler_params=pltpu.CompilerParams(
-                collective_id=0, has_side_effects=True, vmem_limit_bytes=48 * 1024 * 1024),
+                collective_id=0, has_side_effects=True, vmem_limit_bytes=60 * 1024 * 1024),
             cost_estimate=pl.CostEstimate(
                 flops=10 * (halo + 1) * rows * rows * QH * HD, bytes_accessed=9 * rows * QH * HD,
                 transcendentals=(halo + 1) * rows * rows * QH),

time: 61.3 us -> 56.1 us (0.915)
  local copies, waits for them, and re-layouts: 9.72 us -> 3.93 us
  Pallas kernels: 50.6 us -> 51.4 us
    unnamed x19 -> x7, local copies, waits for them, and re-layouts: 9.72 us -> 3.93 us
    pallas_call x1, Pallas kernels: 50.6 us -> 51.4 us  [shards(): pl.pallas_call(functools.partial(kernel, n, grps, halo, pair_rows), out_s...]
where the time goes in v2:
time: 56.1 us; the launch traced here: 56 us
  Pallas kernels  51.4 us (92%)
  local copies, waits for them, and re-layouts  3.93 us (7%)
  between operations  0.65 us (1%)
    pallas_call x1, Pallas kernels, shards(): pl.pallas_call(functools.partial(kernel, n, grps, halo, pair_rows), out_s...  51.4 us
    unnamed x7, local copies, waits for them, and re-layouts  3.93 us

profile of v2, /device:TPU:8, one launch (start us, length us, event | category | flops | bytes accessed | tf_op | source)
XLA Modules:
  0.0 56.0 jit_solution(5565785170998860315)
XLA Ops:
  0.6 51.4 %shard_map.103 = (bf16[1,128,4096]{2,1,0:T(8,128)(2,1)}, bf16[1,128,512]{2,1,0:T(8,128)(2,1)}, bf16[1,128,512]{2,1,0:T(8,128)(2,1)}) custom-call(bf16[1,128,4096]{2,1,0:T(8,128)(2,1)} %q_hbm.1, bf16[1,128,512]{2,1,0:T(8,128)(2,1)} %k_hbm.1, bf16[1,128,512]{2,1,0:T(8,128)(2,1)} %v_hbm.1, bf16[1,128,4096]{2,1,0:T(8,128)(2,1)} %o_hbm.1, ...), custom_call_target="tpu_custom_call" | custom-call | flops 2013265920 | bytes 4718592 | tf_op jit(solution)/shard_map/pallas_call | solution.py:269
  52.0 0.0 copy-start.1
  52.0 2.3 %copy.14 = bf16[1,128,4096]{2,1,0:T(8,128)(2,1)} copy(bf16[1,128,4096]{2,1,0:T(8,128)(2,1)} %get-tuple-element.6) | data formatting | bytes 2097152
  54.4 0.0 copy-done.1
  54.4 0.0 copy-start
  54.4 0.7 %copy.15 = bf16[1,128,512]{2,1,0:T(8,128)(2,1)} copy(bf16[1,128,512]{2,1,0:T(8,128)(2,1)S(1)} %copy-done.1) | data formatting | bytes 262144
  55.0 0.3 copy-done
  55.3 0.7 %copy.16 = bf16[1,128,512]{2,1,0:T(8,128)(2,1)} copy(bf16[1,128,512]{2,1,0:T(8,128)(2,1)S(1)} %copy-done) | data formatting | bytes 262144
Async XLA Ops:
  52.0 2.3 %copy-start.1 = (bf16[1,128,512]{2,1,0:T(8,128)(2,1)S(1)}, bf16[1,128,512]{2,1,0:T(8,128)(2,1)}, u32[]{:S(2)}) copy-start(bf16[1,128,512]{2,1,0:T(8,128)(2,1)} %get-tuple-element.7) | copy-start | bytes 393220
  54.4 1.0 %copy-start = (bf16[1,128,512]{2,1,0:T(8,128)(2,1)S(1)}, bf16[1,128,512]{2,1,0:T(8,128)(2,1)}, u32[]{:S(2)}) copy-start(bf16[1,128,512]{2,1,0:T(8,128)(2,1)} %get-tuple-element.8) | copy-start | bytes 393220

commit v3 on v2

--- a/solution.py
+++ b/solution.py
@@ -13,6 +13,7 @@
 KVH = 4
 SPAN = 8
 GROUP = QH // KVH
+UNIT = 4
 NEGATIVE = -1e30
 MESH = pl.DeviceIdType.MESH
 
@@ -36,7 +37,7 @@
     per_device = rows // SPAN
     slots = halo + 1
     window = slots * rows
-    width = GROUP * HD
+    width, load = UNIT * HD, GROUP * HD
     steps = sorted(range(1, n), key=lambda step: (abs(2 * step - n), step))
     peers = [lax.rem(me + step, n) for step in steps]
     grp_peers = [lax.rem(my_grp + step, grps) for step in range(1, grps)]
@@ -55,7 +56,7 @@
     plan_copy = fetch(plan_hbm, plan_ref, small_in.at[1])
     docs_copy = fetch(docs_hbm, docs_ref, small_in.at[2])
     qog_copies = [
-        [fetch(source.at[0, :, g * width:(g + 1) * width], target.at[:, g * width:(g + 1) * width], qog_in.at[g, i])
+        [fetch(source.at[0, :, g * load:(g + 1) * load], target.at[:, g * load:(g + 1) * load], qog_in.at[g, i])
          for i, (source, target) in enumerate(((q_hbm, q_ref), (o_hbm, o_ref), (g_hbm, g_ref)))]
         for g in range(KVH)
     ]
@@ -104,13 +105,16 @@
 
     for peer in peers:
         count_copy(cnt_ctx, c1_ss, c1_rs, "ctx", me, me, peer).start()
-    for g in range(KVH):
+
+    def send_keys(g):
         for copy in kv_copies[g]:
             copy.wait()
         for s in range(1, halo + 1):
             @pl.when(me + s < n)
             def _():
                 kv_copy(g, s, me + s).start()
+
+    send_keys(0)
 
     plan_copy.wait()
     docs_copy.wait()
@@ -169,13 +173,14 @@
             @pl.when(me < s)
             def _():
                 kvwin[g, :, halo - s] = jnp.zeros((2, rows, HD), jnp.bfloat16)
+        if g + 1 < KVH:
+            send_keys(g + 1)
         for copy in qog_copies[g]:
             copy.wait()
         keys = kvwin[g, 0].reshape(window, HD)
         values = kvwin[g, 1].reshape(window, HD)
         keys_t = jnp.transpose(keys)
-        dk_sum = jnp.zeros((window, HD), jnp.float32)
-        dv_sum = jnp.zeros((window, HD), jnp.float32)
+        stacked = [[], [], [], []]
         for pair in range(GROUP // 2):
             columns = [slice(h * HD, (h + 1) * HD) for h in (g * GROUP + 2 * pair, g * GROUP + 2 * pair + 1)]
             queries = jnp.concatenate([q_ref[:, c] for c in columns], axis=0)
@@ -200,13 +205,18 @@
             dq_half = (dq_t * factor[:, :1]).astype(jnp.bfloat16)
             for i in range(2):
                 packed = dot(pack, dq_half[:, i * rows:(i + 1) * rows], 1, 1).astype(jnp.bfloat16)
-                local = (2 * pair + i) * HD
-                dq_send[g, :, :, local:local + HD] = packed.reshape(n, pair_rows, HD)
-            dk_sum += dot(dscores, queries, 1, 0)
-            dv_sum += dot(probs.astype(jnp.bfloat16), grads, 1, 0)
-        for peer in peers:
-            dq_out(g, peer).start()
-        dq_recv[g, me] = dq_send[g, me]
+                unit, local = divmod(2 * pair + i, UNIT)
+                unit += g * GROUP // UNIT
+                dq_send[unit, :, :, local * HD:(local + 1) * HD] = packed.reshape(n, pair_rows, HD)
+            if local == UNIT - 1:
+                for peer in peers:
+                    dq_out(unit, peer).start()
+                dq_recv[unit, me] = dq_send[unit, me]
+            for pieces, piece in zip(stacked, (dscores, queries, probs.astype(jnp.bfloat16), grads)):
+                pieces.append(piece)
+        all_ds, all_q, all_p, all_g = (jnp.concatenate(x, axis=a) for x, a in zip(stacked, (1, 0, 1, 0)))
+        dk_sum = dot(all_ds, all_q, 1, 0)
+        dv_sum = dot(all_p, all_g, 1, 0)
         for s in range(1, halo + 1):
             at = slice((halo - s) * rows, (halo - s + 1) * rows)
             part_send[g, s - 1, 0] = dk_sum[at].astype(jnp.bfloat16)
@@ -219,6 +229,11 @@
         part_own[g, 1] = dv_sum[halo * rows:]
 
     for g in range(KVH):
+        for unit in range(g * GROUP // UNIT, (g + 1) * GROUP // UNIT):
+            for peer in peers:
+                dq_in(unit, peer).wait_recv()
+            dq_ref[0, :, unit * width:(unit + 1) * width] = dot(
+                unpack, dq_recv[unit].reshape(n * pair_rows, width), 1, 0).astype(jnp.bfloat16)
         for s in range(1, halo + 1):
             @pl.when(me + s < n)
             def _():
@@ -233,10 +248,6 @@
         total = (total * factor[:, :1]).astype(jnp.bfloat16)
         dk_ref[0, :, g * HD:(g + 1) * HD] = total[0]
         dv_ref[0, :, g * HD:(g + 1) * HD] = total[1]
-        for peer in peers:
-            dq_in(g, peer).wait_recv()
-        dq_ref[0, :, g * width:(g + 1) * width] = dot(
-            unpack, dq_recv[g].reshape(n * pair_rows, width), 1, 0).astype(jnp.bfloat16)
 
     for peer in peers:
         count_copy(cnt_ctx, c1_ss, c1_rs, "ctx", me, me, peer).wait_send()
@@ -251,8 +262,9 @@
             @pl.when(me >= s)
             def _():
                 part_copy(g, s, me - s).wait_send()
+    for unit in range(QH // UNIT):
         for peer in peers:
-            dq_out(g, peer).wait_send()
+            dq_out(unit, peer).wait_send()
 
 
 def solution(mesh):
@@ -280,8 +292,8 @@
                 pltpu.VMEM((KVH, halo, 2, rows, HD), bf16),
                 pltpu.VMEM((KVH, halo, 2, rows, HD), bf16),
                 pltpu.VMEM((KVH, 2, rows, HD), f32),
-                pltpu.VMEM((KVH, n, pair_rows, GROUP * HD), bf16),
-                pltpu.VMEM((KVH, n, pair_rows, GROUP * HD), bf16),
+                pltpu.VMEM((QH // UNIT, n, pair_rows, UNIT * HD), bf16),
+                pltpu.VMEM((QH // UNIT, n, pair_rows, UNIT * HD), bf16),
                 pltpu.VMEM((n, 8, 128), f32),
                 pltpu.VMEM((grps, 8, 128), f32),
                 pltpu.VMEM(((halo + 1) * rows, rows), f32),
@@ -294,15 +306,15 @@
                 dma((KVH, 2)), dma((KVH, 3)), dma((3,)),
                 dma((KVH, halo)), dma((KVH, halo)),
                 dma((KVH, halo)), dma((KVH, halo)),
-                dma((KVH, n)), dma((KVH, n)),
+                dma((QH // UNIT, n)), dma((QH // UNIT, n)),
                 dma((n,)), dma((n,)), dma((grps,)), dma((grps,)),
             ],
             compiler_params=pltpu.CompilerParams(
-                collective_id=0, has_side_effects=True, vmem_limit_bytes=60 * 1024 * 1024),
+                collective_id=0, has_side_effects=True, vmem_limit_bytes=40 * 1024 * 1024),
             cost_estimate=pl.CostEstimate(
                 flops=10 * (halo + 1) * rows * rows * QH * HD, bytes_accessed=9 * rows * QH * HD,
                 transcendentals=(halo + 1) * rows * rows * QH),
-        )(*args)
+        )(*[pltpu.with_memory_space_constraint(a, pltpu.HBM) for a in args])
 
     in_specs = (
         P("grp", "ctx", None),

time: 56.1 us -> 52.1 us (0.929)
  Pallas kernels: 51.4 us -> 49 us
  local copies, waits for them, and re-layouts: 3.93 us -> 2.28 us
    pallas_call x1, Pallas kernels: 51.4 us -> 49 us  [shards(): pl.pallas_call(functools.partial(kernel, n, grps, halo, pair_rows), out_s...]
    unnamed x7 -> x3, local copies, waits for them, and re-layouts: 3.93 us -> 2.28 us
where the time goes in v3:
time: 52.1 us; the launch traced here: 51.9 us
  Pallas kernels  49 us (94%)
  local copies, waits for them, and re-layouts  2.28 us (4%)
  between operations  0.64 us (1%)
    pallas_call x1, Pallas kernels, shards(): pl.pallas_call(functools.partial(kernel, n, grps, halo, pair_rows), out_s...  49 us
    unnamed x3, local copies, waits for them, and re-layouts  2.28 us

profile of v3, /device:TPU:8, one launch (start us, length us, event | category | flops | bytes accessed | tf_op | source)
XLA Modules:
  0.0 51.9 jit_solution(9357746238959806605)
XLA Ops:
  0.6 49.0 %shard_map.103 = (bf16[1,128,4096]{2,1,0:T(8,128)(2,1)S(1)}, bf16[1,128,512]{2,1,0:T(8,128)(2,1)S(1)}, bf16[1,128,512]{2,1,0:T(8,128)(2,1)S(1)}) custom-call(bf16[1,128,4096]{2,1,0:T(8,128)(2,1)} %q_hbm.1, bf16[1,128,512]{2,1,0:T(8,128)(2,1)} %k_hbm.1, bf16[1,128,512]{2,1,0:T(8,128)(2,1)} %v_hbm.1, bf16[1,128,4096]{2,1,0:T(8,128)(2,1)} %o_hbm.1, ...), custom_call_target="tpu_custom_call" | custom-call | flops 2013265920 | bytes 4718592 | tf_op jit(solution)/shard_map/pallas_call | solution.py:281
  49.6 1.0 %copy.14 = bf16[1,128,4096]{2,1,0:T(8,128)(2,1)} copy(bf16[1,128,4096]{2,1,0:T(8,128)(2,1)S(1)} %get-tuple-element.6) | data formatting | bytes 2097152
  50.6 0.7 %copy.15 = bf16[1,128,512]{2,1,0:T(8,128)(2,1)} copy(bf16[1,128,512]{2,1,0:T(8,128)(2,1)S(1)} %get-tuple-element.7) | data formatting | bytes 262144
  51.3 0.7 %copy.16 = bf16[1,128,512]{2,1,0:T(8,128)(2,1)} copy(bf16[1,128,512]{2,1,0:T(8,128)(2,1)S(1)} %get-tuple-element.8) | data formatting | bytes 262144

commit v4 on v3

--- a/solution.py
+++ b/solution.py
@@ -13,7 +13,7 @@
 KVH = 4
 SPAN = 8
 GROUP = QH // KVH
-UNIT = 4
+UNIT = 2
 NEGATIVE = -1e30
 MESH = pl.DeviceIdType.MESH
 

time: 52.1 us -> 52.9 us (1.015)
  Pallas kernels: 49 us -> 49.8 us
    pallas_call x1, Pallas kernels: 49 us -> 49.8 us  [shards(): pl.pallas_call(functools.partial(kernel, n, grps, halo, pair_rows), out_s...]
where the time goes in v4:
time: 52.9 us; the launch traced here: 52.7 us
  Pallas kernels  49.8 us (94%)
  local copies, waits for them, and re-layouts  2.28 us (4%)
  between operations  0.64 us (1%)
    pallas_call x1, Pallas kernels, shards(): pl.pallas_call(functools.partial(kernel, n, grps, halo, pair_rows), out_s...  49.8 us
    unnamed x3, local copies, waits for them, and re-layouts  2.28 us

profile of v4, /device:TPU:8, one launch (start us, length us, event | category | flops | bytes accessed | tf_op | source)
XLA Modules:
  0.0 52.7 jit_solution(6369530417211953460)
XLA Ops:
  0.6 49.8 %shard_map.103 = (bf16[1,128,4096]{2,1,0:T(8,128)(2,1)S(1)}, bf16[1,128,512]{2,1,0:T(8,128)(2,1)S(1)}, bf16[1,128,512]{2,1,0:T(8,128)(2,1)S(1)}) custom-call(bf16[1,128,4096]{2,1,0:T(8,128)(2,1)} %q_hbm.1, bf16[1,128,512]{2,1,0:T(8,128)(2,1)} %k_hbm.1, bf16[1,128,512]{2,1,0:T(8,128)(2,1)} %v_hbm.1, bf16[1,128,4096]{2,1,0:T(8,128)(2,1)} %o_hbm.1, ...), custom_call_target="tpu_custom_call" | custom-call | flops 2013265920 | bytes 4718592 | tf_op jit(solution)/shard_map/pallas_call | solution.py:281
  50.4 1.0 %copy.14 = bf16[1,128,4096]{2,1,0:T(8,128)(2,1)} copy(bf16[1,128,4096]{2,1,0:T(8,128)(2,1)S(1)} %get-tuple-element.6) | data formatting | bytes 2097152
  51.4 0.7 %copy.15 = bf16[1,128,512]{2,1,0:T(8,128)(2,1)} copy(bf16[1,128,512]{2,1,0:T(8,128)(2,1)S(1)} %get-tuple-element.7) | data formatting | bytes 262144
  52.0 0.7 %copy.16 = bf16[1,128,512]{2,1,0:T(8,128)(2,1)} copy(bf16[1,128,512]{2,1,0:T(8,128)(2,1)S(1)} %get-tuple-element.8) | data formatting | bytes 262144
